TPU v7x, 32 devices: a whole 2x2x4 slice. The times are simulated.
32 devices in a mesh: seq: 8 (over z, y), chan: 4 (over x, core).
Axes of the slice: x: 2, y: 2, z: 4, core: 2. Of those that a mesh axis runs over, the one named last changes fastest.
Arguments:
- query_gate: float32 [16, 65536], P('chan', 'seq'), may hold values from -6 to 6
- key_gate: float32 [16, 65536], P('chan', 'seq'), may hold values from -6 to 6
- value_input: float32 [16, 65536], P('chan', 'seq'), may hold values from -6 to 6
- filter_taps: float32 [4, 65536], P(None, ('seq', 'chan')), may hold values from -2 to 2
- cotangent: float32 [16, 65536], P('chan', 'seq'), may hold values from -6 to 6
Outputs:
- query_grad: float32 [16, 65536], P('chan', 'seq')
- key_grad: float32 [16, 65536], P('chan', 'seq')
- value_grad: float32 [16, 65536], P('chan', 'seq')
All inputs are finite; a program needn't handle non-finite values.
Results may differ from a plain program's by a relative error of at most 0.00013.
Values sent between devices are 32-bit elements; how exact they have to be, the bound alone decides.
A program may use at most 64 MiB of HBM per device.

v0:
```python
from functools import partial
import math

import jax
import jax.numpy as jnp
from jax import lax
from jax.sharding import PartitionSpec as P


def phase_table(row_count, column_count, offset, period, direction):
    row_index = lax.broadcasted_iota(jnp.int32, (row_count, column_count), 0)
    column_index = lax.broadcasted_iota(jnp.int32, (row_count, column_count), 1)
    phases = row_index * (column_index + offset) % period
    angles = phases.astype(jnp.float32) * (direction * 2.0 * math.pi / period)
    return (jnp.cos(angles), jnp.sin(angles))


def complex_mix(formula, table_real, table_imag, data_real, data_imag):
    product = partial(jnp.einsum, formula, precision=lax.Precision.HIGHEST)
    return (
        product(table_real, data_real) - product(table_imag, data_imag),
        product(table_real, data_imag) + product(table_imag, data_real),
    )


def regroup_tokens(signal):
    return lax.all_to_all(signal, "seq", split_axis=1, concat_axis=1, tiled=True)


def regroup_spectrum(part_real, part_imag):
    return (
        lax.all_to_all(part_real, "seq", split_axis=1, concat_axis=1, tiled=True),
        lax.all_to_all(part_imag, "seq", split_axis=1, concat_axis=1, tiled=True),
    )


def finish_forward(moved_real, moved_imag, blocks, width, tokens):
    outer_real, outer_imag = phase_table(blocks, blocks, 0, blocks, -1.0)
    coarse_real, coarse_imag = complex_mix(
        "ur,crjq->cujq", outer_real, outer_imag, moved_real, moved_imag
    )
    shift_real, shift_imag = phase_table(blocks, width, 0, tokens, -1.0)
    shift_real = shift_real[None, :, None, :]
    shift_imag = shift_imag[None, :, None, :]
    twisted_real = coarse_real * shift_real - coarse_imag * shift_imag
    twisted_imag = coarse_real * shift_imag + coarse_imag * shift_real
    inner_real, inner_imag = phase_table(width, width, 0, width, -1.0)
    return complex_mix("qv,cujq->cujv", inner_real, inner_imag, twisted_real, twisted_imag)


def start_inverse(spectrum_real, spectrum_imag, blocks, width, tokens):
    inner_real, inner_imag = phase_table(width, width, 0, width, 1.0)
    fine_real, fine_imag = complex_mix(
        "vq,cujv->cujq", inner_real, inner_imag, spectrum_real, spectrum_imag
    )
    shift_real, shift_imag = phase_table(blocks, width, 0, tokens, 1.0)
    shift_real = shift_real[None, :, None, :]
    shift_imag = shift_imag[None, :, None, :]
    untwisted_real = fine_real * shift_real - fine_imag * shift_imag
    untwisted_imag = fine_real * shift_imag + fine_imag * shift_real
    outer_real, outer_imag = phase_table(blocks, blocks, 0, blocks, 1.0)
    return complex_mix("ru,cujq->crjq", outer_real, outer_imag, untwisted_real, untwisted_imag)


def forward_spectrum(signal):
    count, tokens = signal.shape
    blocks = lax.axis_size("seq")
    width = tokens // blocks
    freqs = 2 * blocks
    period = freqs * tokens
    rank = lax.axis_index("seq")
    gathered = regroup_tokens(signal.reshape(count, blocks, width))
    product = partial(jnp.einsum, "kp,cpq->ckq", precision=lax.Precision.HIGHEST)
    anchor = rank * width
    first_real, first_imag = phase_table(freqs, blocks, 0, freqs, -1.0)
    mixed_real = product(first_real, gathered)
    mixed_imag = product(first_imag, gathered)
    turn_real, turn_imag = phase_table(freqs, width, anchor, period, -1.0)
    moved_real, moved_imag = regroup_spectrum(
        mixed_real * turn_real - mixed_imag * turn_imag,
        mixed_real * turn_imag + mixed_imag * turn_real,
    )
    moved_real = moved_real.reshape(count, blocks, 2, width)
    moved_imag = moved_imag.reshape(count, blocks, 2, width)
    return finish_forward(moved_real, moved_imag, blocks, width, tokens)


def inverse_spectrum(spectrum_real, spectrum_imag):
    count, blocks, per_device, width = spectrum_real.shape
    tokens = blocks * width
    freqs = 2 * blocks
    period = freqs * tokens
    rank = lax.axis_index("seq")
    spread_real, spread_imag = start_inverse(spectrum_real, spectrum_imag, blocks, width, tokens)
    product = partial(jnp.einsum, "kp,ckq->cpq", precision=lax.Precision.HIGHEST)
    anchor = rank * width
    moved_real, moved_imag = regroup_spectrum(
        spread_real.reshape(count, blocks * per_device, width),
        spread_imag.reshape(count, blocks * per_device, width),
    )
    turn_real, turn_imag = phase_table(freqs, width, anchor, period, 1.0)
    level_real = moved_real * turn_real - moved_imag * turn_imag
    level_imag = moved_real * turn_imag + moved_imag * turn_real
    first_real, first_imag = phase_table(freqs, blocks, 0, freqs, 1.0)
    rebuilt = (product(first_real, level_real) - product(first_imag, level_imag)) * (1.0 / period)
    return regroup_tokens(rebuilt).reshape(count, tokens)


def on_device(query_gate, key_gate, value_input, filter_taps, cotangent):
    block_taps = lax.all_gather(filter_taps, "chan", axis=1, tiled=True)
    filter_real, filter_imag = forward_spectrum(block_taps)
    gated = key_gate * value_input
    weighted = cotangent * query_gate
    gated_real, gated_imag = forward_spectrum(gated)
    convolved = inverse_spectrum(
        gated_real * filter_real - gated_imag * filter_imag,
        gated_real * filter_imag + gated_imag * filter_real,
    )
    weighted_real, weighted_imag = forward_spectrum(weighted)
    gated_grad = inverse_spectrum(
        weighted_real * filter_real + weighted_imag * filter_imag,
        weighted_imag * filter_real - weighted_real * filter_imag,
    )
    return (cotangent * convolved, gated_grad * value_input, gated_grad * key_gate)


def solution(mesh):
    in_specs = (
        P("chan", "seq"),
        P("chan", "seq"),
        P("chan", "seq"),
        P(None, ("seq", "chan")),
        P("chan", "seq"),
    )
    out_specs = (P("chan", "seq"), P("chan", "seq"), P("chan", "seq"))
    return jax.shard_map(
        on_device, mesh=mesh, in_specs=in_specs, out_specs=out_specs, check_vma=False
    )
```

profile of v0, /device:TPU:0, one launch (start us, length us, event | category | flops | bytes accessed | tf_op | source)
XLA Modules:
  0.0 542.9 jit_solution(3062477605782335945)
XLA Ops:
  2.3 7.4 %all-to-all-start = ((f32[4,8,1024]{2,0,1:T(4,128)}), f32[4,8,1024]{2,0,1:T(4,128)S(1)}, u32[]{:S(2)}, u32[]{:S(2)}) async-start(f32[4,8,1024]{2,0,1:T(4,128)} %bitcast), calls=%async_computation | async-start | bytes 262144 | tf_op jit(solution)/shard_map/all_to_all | solution.py:27
  92.8 18.3 %fusion.28 = f32[4,8,2,1024]{3,1,2,0:T(8,128)S(1)} fusion(f32[4,8,2,1024]{3,1,2,0:T(8,128)S(1)} %fusion.69, f32[4,8,2,1024]{3,1,2,0:T(8,128)S(1)} %fusion.70, f32[8,1024]{1,0:T(8,128)S(1)} %get-tuple-element.29, f32[8,1024]{1,0:T(8,128)S(1)} %get-tuple-element.30), kind=kOutput, calls=%fused_computation.31 | convolution fusion | flops 820183040 | bytes 851968 | tf_op jit(solution)/shard_map/qv,cujq->cujv/dot_general | solution.py:21
  111.1 18.3 %fusion.24 = f32[4,8,2,1024]{3,1,2,0:T(8,128)S(1)} fusion(f32[4,8,2,1024]{3,1,2,0:T(8,128)S(1)} %fusion.69, f32[4,8,2,1024]{3,1,2,0:T(8,128)S(1)} %fusion.70, f32[8,1024]{1,0:T(8,128)S(1)} %get-tuple-element.29, f32[8,1024]{1,0:T(8,128)S(1)} %get-tuple-element.30), kind=kOutput, calls=%fused_computation.27 | convolution fusion | flops 820183040 | bytes 851968 | tf_op jit(solution)/shard_map/qv,cujq->cujv/dot_general | solution.py:22
  136.2 18.3 %fusion.26 = f32[4,8,2,1024]{3,1,2,0:T(8,128)S(1)} fusion(f32[4,8,2,1024]{3,1,2,0:T(8,128)S(1)} %fusion.67, f32[4,8,2,1024]{3,1,2,0:T(8,128)S(1)} %fusion.68, f32[8,1024]{1,0:T(8,128)S(1)} %get-tuple-element.29, f32[8,1024]{1,0:T(8,128)S(1)} %get-tuple-element.30), kind=kOutput, calls=%fused_computation.29 | convolution fusion | flops 820183040 | bytes 851968 | tf_op jit(solution)/shard_map/qv,cujq->cujv/dot_general | solution.py:21
  154.5 18.3 %fusion.22 = f32[4,8,2,1024]{3,1,2,0:T(8,128)S(1)} fusion(f32[4,8,2,1024]{3,1,2,0:T(8,128)S(1)} %fusion.67, f32[4,8,2,1024]{3,1,2,0:T(8,128)S(1)} %fusion.68, f32[8,1024]{1,0:T(8,128)S(1)} %get-tuple-element.29, f32[8,1024]{1,0:T(8,128)S(1)} %get-tuple-element.30), kind=kOutput, calls=%fused_computation.25 | convolution fusion | flops 820183040 | bytes 851968 | tf_op jit(solution)/shard_map/qv,cujq->cujv/dot_general | solution.py:22
  174.4 18.5 %fusion.18 = f32[4,8,2,1024]{3,1,2,0:T(8,128)S(1)} fusion(f32[4,8,2,1024]{3,1,2,0:T(8,128)S(1)} %fusion.63, f32[4,8,2,1024]{3,1,2,0:T(8,128)S(1)} %fusion.64, f32[8,1024]{1,0:T(8,128)S(1)} %get-tuple-element.29, f32[8,1024]{1,0:T(8,128)S(1)} %get-tuple-element.30), kind=kOutput, calls=%fused_computation.21 | convolution fusion | flops 820183040 | bytes 851968 | tf_op jit(solution)/shard_map/qv,cujq->cujv/dot_general | solution.py:22
  193.0 18.3 %fusion.20 = f32[4,8,2,1024]{3,1,2,0:T(8,128)S(1)} fusion(f32[4,8,2,1024]{3,1,2,0:T(8,128)S(1)} %fusion.63, f32[4,8,2,1024]{3,1,2,0:T(8,128)S(1)} %fusion.64, f32[8,1024]{1,0:T(8,128)S(1)} %get-tuple-element.29, f32[8,1024]{1,0:T(8,128)S(1)} %get-tuple-element.30), kind=kOutput, calls=%fused_computation.23 | convolution fusion | flops 820183040 | bytes 851968 | tf_op jit(solution)/shard_map/qv,cujq->cujv/dot_general | solution.py:21
  211.3 18.6 %fusion.71 = f32[4,8,2,1024]{3,1,2,0:T(8,128)S(1)} fusion(f32[4,8,2,1024]{3,1,2,0:T(8,128)S(1)} %fusion.28, f32[4,8,2,1024]{3,1,2,0:T(8,128)S(1)} %fusion.69, f32[4,8,2,1024]{3,1,2,0:T(8,128)S(1)} %fusion.70, f32[8,1024]{1,0:T(8,128)S(1)} %get-tuple-element.29, f32[8,1024]{1,0:T(8,128)S(1)} %get-tuple-element.30), kind=kOutput, calls=%fused_computation.84 | convolution fusion | flops 820248576 | bytes 1114112 | tf_op jit(solution)/shard_map/qv,cujq->cujv/dot_general | solution.py:21
  229.9 18.2 %fusion.77 = f32[4,8,2,1024]{3,1,2,0:T(8,128)S(1)} fusion(f32[4,8,2,1024]{3,1,2,0:T(8,128)S(1)} %fusion.24, f32[4,8,2,1024]{3,1,2,0:T(8,128)S(1)} %fusion.69, f32[4,8,2,1024]{3,1,2,0:T(8,128)S(1)} %fusion.70, f32[8,1024]{1,0:T(8,128)S(1)} %get-tuple-element.29, f32[8,1024]{1,0:T(8,128)S(1)} %get-tuple-element.30), kind=kOutput, calls=%fused_computation.86 | convolution fusion | flops 820248576 | bytes 1114112 | tf_op jit(solution)/shard_map/qv,cujq->cujv/dot_general | solution.py:22
  248.0 18.3 %fusion.74 = f32[4,8,2,1024]{3,1,2,0:T(8,128)S(1)} fusion(f32[4,8,2,1024]{3,1,2,0:T(8,128)S(1)} %fusion.26, f32[4,8,2,1024]{3,1,2,0:T(8,128)S(1)} %fusion.67, f32[4,8,2,1024]{3,1,2,0:T(8,128)S(1)} %fusion.68, f32[8,1024]{1,0:T(8,128)S(1)} %get-tuple-element.29, f32[8,1024]{1,0:T(8,128)S(1)} %get-tuple-element.30), kind=kOutput, calls=%fused_computation.85 | convolution fusion | flops 820248576 | bytes 1114112 | tf_op jit(solution)/shard_map/qv,cujq->cujv/dot_general | solution.py:21
  266.4 18.1 %fusion.86 = f32[4,8,2,1024]{3,1,2,0:T(8,128)S(1)} fusion(f32[4,8,2,1024]{3,1,2,0:T(8,128)S(1)} %fusion.18, f32[4,8,2,1024]{3,1,2,0:T(8,128)S(1)} %fusion.63, f32[4,8,2,1024]{3,1,2,0:T(8,128)S(1)} %fusion.64, f32[8,1024]{1,0:T(8,128)S(1)} %get-tuple-element.29, f32[8,1024]{1,0:T(8,128)S(1)} %get-tuple-element.30), kind=kOutput, calls=%fused_computation.89 | convolution fusion | flops 820248576 | bytes 1114112 | tf_op jit(solution)/shard_map/qv,cujq->cujv/dot_general | solution.py:22
  284.5 18.4 %fusion.80 = f32[4,8,2,1024]{3,1,2,0:T(8,128)S(1)} fusion(f32[4,8,2,1024]{3,1,2,0:T(8,128)S(1)} %fusion.22, f32[4,8,2,1024]{3,1,2,0:T(8,128)S(1)} %fusion.67, f32[4,8,2,1024]{3,1,2,0:T(8,128)S(1)} %fusion.68, f32[8,1024]{1,0:T(8,128)S(1)} %get-tuple-element.29, f32[8,1024]{1,0:T(8,128)S(1)} %get-tuple-element.30), kind=kOutput, calls=%fused_computation.87 | convolution fusion | flops 820248576 | bytes 1114112 | tf_op jit(solution)/shard_map/qv,cujq->cujv/dot_general | solution.py:22
  302.9 18.3 %multiply_subtract_fusion.2 = (f32[4,8,2,1024]{3,1,2,0:T(8,128)S(1)}, f32[4,8,2,1024]{3,1,2,0:T(8,128)S(1)}, f32[4,8,2,1024]{3,1,2,0:T(8,128)S(1)}, f32[4,8,2,1024]{3,1,2,0:T(8,128)S(1)}) fusion(f32[4,8,2,1024]{3,1,2,0:T(8,128)S(1)} %fusion.80, f32[4,8,2,1024]{3,1,2,0:T(8,128)S(1)} %fusion.86, f32[4,8,2,1024]{3,1,2,0:T(8,128)S(1)} %fusion.74, ...), kind=kOutput, calls=%fused_computation.110 | convolution fusion | flops 821035008 | bytes 3211264 | tf_op jit(solution)/shard_map/qv,cujq->cujv/dot_general | solution.py:21
  321.2 18.7 %fusion.8 = f32[4,8,2,1024]{3,1,2,0:T(8,128)S(1)} fusion(f32[4,8,2,1024]{3,1,2,0:T(8,128)S(1)} %get-tuple-element.18), kind=kOutput, calls=%fused_computation.11 | convolution fusion | flops 819986432 | bytes 524288 | tf_op jit(solution)/shard_map/vq,cujv->cujq/dot_general | solution.py:21
  339.8 18.2 %fusion.6 = f32[4,8,2,1024]{3,1,2,0:T(8,128)S(1)} fusion(f32[4,8,2,1024]{3,1,2,0:T(8,128)S(1)} %get-tuple-element.17), kind=kOutput, calls=%fused_computation.9 | convolution fusion | flops 819986432 | bytes 524288 | tf_op jit(solution)/shard_map/vq,cujv->cujq/dot_general | solution.py:22
  358.1 18.3 %fusion.89 = f32[4,8,2,1024]{3,1,2,0:T(8,128)S(1)} fusion(f32[4,8,2,1024]{3,1,2,0:T(8,128)S(1)} %fusion.8, f32[4,8,2,1024]{3,1,2,0:T(8,128)S(1)} %get-tuple-element.17), kind=kOutput, calls=%fused_computation.90 | convolution fusion | flops 820051968 | bytes 786432 | tf_op jit(solution)/shard_map/vq,cujv->cujq/dot_general | solution.py:21
  376.4 18.1 %fusion.92 = f32[4,8,2,1024]{3,1,2,0:T(8,128)S(1)} fusion(f32[4,8,2,1024]{3,1,2,0:T(8,128)S(1)} %fusion.6, f32[4,8,2,1024]{3,1,2,0:T(8,128)S(1)} %get-tuple-element.18), kind=kOutput, calls=%fused_computation.91 | convolution fusion | flops 820051968 | bytes 786432 | tf_op jit(solution)/shard_map/vq,cujv->cujq/dot_general | solution.py:22
  404.1 18.2 %fusion.4 = f32[4,8,2,1024]{3,1,2,0:T(8,128)S(1)} fusion(f32[4,8,2,1024]{3,1,2,0:T(8,128)S(1)} %get-tuple-element.3), kind=kOutput, calls=%fused_computation.7 | convolution fusion | flops 819986432 | bytes 524288 | tf_op jit(solution)/shard_map/vq,cujv->cujq/dot_general | solution.py:21
  422.3 18.2 %fusion.2 = f32[4,8,2,1024]{3,1,2,0:T(8,128)S(1)} fusion(f32[4,8,2,1024]{3,1,2,0:T(8,128)S(1)} %get-tuple-element.4), kind=kOutput, calls=%fused_computation.5 | convolution fusion | flops 819986432 | bytes 524288 | tf_op jit(solution)/shard_map/vq,cujv->cujq/dot_general | solution.py:22
  440.6 18.3 %fusion.95 = f32[4,8,2,1024]{3,1,2,0:T(8,128)S(1)} fusion(f32[4,8,2,1024]{3,1,2,0:T(8,128)S(1)} %fusion.4, f32[4,8,2,1024]{3,1,2,0:T(8,128)S(1)} %get-tuple-element.4), kind=kOutput, calls=%fused_computation.92 | convolution fusion | flops 820051968 | bytes 786432 | tf_op jit(solution)/shard_map/vq,cujv->cujq/dot_general | solution.py:21
  458.9 18.1 %fusion.98 = f32[4,8,2,1024]{3,1,2,0:T(8,128)S(1)} fusion(f32[4,8,2,1024]{3,1,2,0:T(8,128)S(1)} %fusion.2, f32[4,8,2,1024]{3,1,2,0:T(8,128)S(1)} %get-tuple-element.3), kind=kOutput, calls=%fused_computation.93 | convolution fusion | flops 820051968 | bytes 786432 | tf_op jit(solution)/shard_map/vq,cujv->cujq/dot_general | solution.py:22
  484.7 7.4 %all-to-all-done.7 = f32[4,16,1024]{2,0,1:T(4,128)S(1)} async-done(((f32[4,16,1024]{2,0,1:T(4,128)}), f32[4,16,1024]{2,0,1:T(4,128)S(1)}, u32[]{:S(2)}, u32[]{:S(2)}) %all-to-all-start.7) | async-done | bytes 262176 | tf_op jit(solution)/shard_map/all_to_all | solution.py:33
  497.8 8.0 %all-to-all-done.12 = f32[4,16,1024]{2,0,1:T(4,128)S(1)} async-done(((f32[4,16,1024]{2,0,1:T(4,128)}), f32[4,16,1024]{2,0,1:T(4,128)S(1)}, u32[]{:S(2)}, u32[]{:S(2)}) %all-to-all-start.12) | async-done | bytes 262176 | tf_op jit(solution)/shard_map/all_to_all | solution.py:32
  505.8 12.7 %all_to_all.75 = f32[4,16,1024]{2,0,1:T(4,128)S(1)} all-to-all(f32[4,16,1024]{2,0,1:T(4,128)S(1)} %bitcast.225), channel_id=1, replica_groups=mesh['seq'=8,'chan'=4] {'seq'}, dimensions={1} | all-to-all | bytes 524288 | tf_op jit(solution)/shard_map/all_to_all | solution.py:33
  (87 shorter events, 139.6 us)
Async XLA Ops:
  0.6 9.1 %copy-start.4 = (f32[4,2048]{1,0:T(4,128)S(1)}, f32[4,2048]{1,0:T(4,128)}, u32[]{:S(2)}) copy-start(f32[4,2048]{1,0:T(4,128)} %param.8) | copy-start | bytes 98308
  2.3 13.3 %copy-start.2 = (f32[4,8192]{1,0:T(4,128)S(1)}, f32[4,8192]{1,0:T(4,128)}, u32[]{:S(2)}) copy-start(f32[4,8192]{1,0:T(4,128)} %param.9) | copy-start | bytes 393220
  2.3 13.3 %copy-start.3 = (f32[4,8192]{1,0:T(4,128)S(1)}, f32[4,8192]{1,0:T(4,128)}, u32[]{:S(2)}) copy-start(f32[4,8192]{1,0:T(4,128)} %param.5) | copy-start | bytes 393220
  2.3 14.8 %all-to-all-start = ((f32[4,8,1024]{2,0,1:T(4,128)}), f32[4,8,1024]{2,0,1:T(4,128)S(1)}, u32[]{:S(2)}, u32[]{:S(2)}) async-start(f32[4,8,1024]{2,0,1:T(4,128)} %bitcast), calls=%async_computation | async-start | bytes 262144 | tf_op jit(solution)/shard_map/all_to_all | solution.py:27
  17.1 13.2 %all-to-all-start.9 = ((f32[4,8,1024]{2,0,1:T(4,128)}), f32[4,8,1024]{2,0,1:T(4,128)S(1)}, u32[]{:S(2)}, u32[]{:S(2)}) async-start(f32[4,8,1024]{2,0,1:T(4,128)} %bitcast.48), calls=%async_computation.9 | async-start | bytes 262144 | tf_op jit(solution)/shard_map/all_to_all | solution.py:27
  30.3 10.7 %all-to-all-start.3 = ((f32[4,8,1024]{2,0,1:T(4,128)}), f32[4,8,1024]{2,0,1:T(4,128)S(1)}, u32[]{:S(2)}, u32[]{:S(2)}) async-start(f32[4,8,1024]{2,0,1:T(4,128)} %bitcast.19), calls=%async_computation.3 | async-start | bytes 262144 | tf_op jit(solution)/shard_map/all_to_all | solution.py:27
  41.0 11.6 %all-to-all-start.2 = ((f32[4,16,1024]{2,0,1:T(4,128)}), f32[4,16,1024]{2,0,1:T(4,128)S(1)}, u32[]{:S(2)}, u32[]{:S(2)}) async-start(f32[4,16,1024]{2,0,1:T(4,128)} %copy.66), calls=%async_computation.2 | async-start | bytes 524288 | tf_op jit(solution)/shard_map/all_to_all | solution.py:33
  52.5 11.6 %all-to-all-start.1 = ((f32[4,16,1024]{2,0,1:T(4,128)}), f32[4,16,1024]{2,0,1:T(4,128)S(1)}, u32[]{:S(2)}, u32[]{:S(2)}) async-start(f32[4,16,1024]{2,0,1:T(4,128)} %copy.64), calls=%async_computation.1 | async-start | bytes 524288 | tf_op jit(solution)/shard_map/all_to_all | solution.py:32
  64.1 11.6 %all-to-all-start.4 = ((f32[4,16,1024]{2,0,1:T(4,128)}), f32[4,16,1024]{2,0,1:T(4,128)S(1)}, u32[]{:S(2)}, u32[]{:S(2)}) async-start(f32[4,16,1024]{2,0,1:T(4,128)} %copy.72), calls=%async_computation.4 | async-start | bytes 524288 | tf_op jit(solution)/shard_map/all_to_all | solution.py:32
  75.7 11.6 %all-to-all-start.5 = ((f32[4,16,1024]{2,0,1:T(4,128)}), f32[4,16,1024]{2,0,1:T(4,128)S(1)}, u32[]{:S(2)}, u32[]{:S(2)}) async-start(f32[4,16,1024]{2,0,1:T(4,128)} %copy.74), calls=%async_computation.5 | async-start | bytes 524288 | tf_op jit(solution)/shard_map/all_to_all | solution.py:33
  87.3 42.1 %all-to-all-start.10 = ((f32[4,16,1024]{2,0,1:T(4,128)}), f32[4,16,1024]{2,0,1:T(4,128)S(1)}, u32[]{:S(2)}, u32[]{:S(2)}) async-start(f32[4,16,1024]{2,0,1:T(4,128)} %copy.85), calls=%async_computation.10 | async-start | bytes 524288 | tf_op jit(solution)/shard_map/all_to_all | solution.py:32
  129.5 43.4 %all-to-all-start.11 = ((f32[4,16,1024]{2,0,1:T(4,128)}), f32[4,16,1024]{2,0,1:T(4,128)S(1)}, u32[]{:S(2)}, u32[]{:S(2)}) async-start(f32[4,16,1024]{2,0,1:T(4,128)} %copy.87), calls=%async_computation.11 | async-start | bytes 524288 | tf_op jit(solution)/shard_map/all_to_all | solution.py:33
  396.6 80.5 %all-to-all-start.6 = ((f32[4,16,1024]{2,0,1:T(4,128)}), f32[4,16,1024]{2,0,1:T(4,128)S(1)}, u32[]{:S(2)}, u32[]{:S(2)}) async-start(f32[4,16,1024]{2,0,1:T(4,128)} %bitcast.39), calls=%async_computation.6 | async-start | bytes 524288 | tf_op jit(solution)/shard_map/all_to_all | solution.py:32
  477.0 15.1 %all-to-all-start.7 = ((f32[4,16,1024]{2,0,1:T(4,128)}), f32[4,16,1024]{2,0,1:T(4,128)S(1)}, u32[]{:S(2)}, u32[]{:S(2)}) async-start(f32[4,16,1024]{2,0,1:T(4,128)} %bitcast.43), calls=%async_computation.7 | async-start | bytes 524288 | tf_op jit(solution)/shard_map/all_to_all | solution.py:33
  492.1 13.6 %all-to-all-start.12 = ((f32[4,16,1024]{2,0,1:T(4,128)}), f32[4,16,1024]{2,0,1:T(4,128)S(1)}, u32[]{:S(2)}, u32[]{:S(2)}) async-start(f32[4,16,1024]{2,0,1:T(4,128)} %bitcast.56), calls=%async_computation.12 | async-start | bytes 524288 | tf_op jit(solution)/shard_map/all_to_all | solution.py:32
  520.4 10.7 %all-to-all-start.14 = ((f32[4,8,1024]{2,0,1:T(4,128)}), f32[4,8,1024]{2,0,1:T(4,128)S(1)}, u32[]{:S(2)}, u32[]{:S(2)}) async-start(f32[4,8,1024]{2,0,1:T(4,128)} %copy.95), calls=%async_computation.14 | async-start | bytes 262144 | tf_op jit(solution)/shard_map/all_to_all | solution.py:27
  524.7 9.8 %copy-start = (f32[4,8192]{1,0:T(4,128)S(1)}, f32[4,8192]{1,0:T(4,128)}, u32[]{:S(2)}) copy-start(f32[4,8192]{1,0:T(4,128)} %param.6) | copy-start | bytes 393220
  524.7 9.8 %copy-start.1 = (f32[4,8192]{1,0:T(4,128)S(1)}, f32[4,8192]{1,0:T(4,128)}, u32[]{:S(2)}) copy-start(f32[4,8192]{1,0:T(4,128)} %param.7) | copy-start | bytes 393220
  531.1 10.7 %all-to-all-start.8 = ((f32[4,8,1024]{2,0,1:T(4,128)}), f32[4,8,1024]{2,0,1:T(4,128)S(1)}, u32[]{:S(2)}, u32[]{:S(2)}) async-start(f32[4,8,1024]{2,0,1:T(4,128)} %copy.82), calls=%async_computation.8 | async-start | bytes 262144 | tf_op jit(solution)/shard_map/all_to_all | solution.py:27
where the time goes:
time: 550 us; the launch traced here: 543 us
  matrix products  380 us (69%)
  waiting for transfers between devices  64.1 us (12%)
  starting transfers between devices  63.9 us (12%)
  blocking collectives  18.5 us (3%)
  local copies, waits for them, and re-layouts  9.55 us (2%)
    dot_general x10, matrix products, complex_mix(): product(table_imag, data_imag)  94.2 us
    dot_general x10, matrix products, complex_mix(): product(table_real, data_real) - product(table_imag, data_imag)  94.1 us
    dot_general x10, matrix products, complex_mix(): product(table_imag, data_real)  94.1 us
    dot_general x10, matrix products, complex_mix(): product(table_real, data_imag) + product(table_imag, data_real)  93.2 us
    all_to_all x5, waiting for transfers between devices, regroup_tokens(): lax.all_to_all(signal, 'seq', split_axis=1, concat_axis=1, tiled=True)  24.3 us
    all_to_all x5, starting transfers between devices, regroup_tokens(): lax.all_to_all(signal, 'seq', split_axis=1, concat_axis=1, tiled=True)  23.3 us
    all_to_all x5, starting transfers between devices, regroup_spectrum(): lax.all_to_all(part_real, 'seq', split_axis=1, concat_axis=1, tiled=True)  21.6 us
    all_to_all x4, waiting for transfers between devices, regroup_spectrum(): lax.all_to_all(part_imag, 'seq', split_axis=1, concat_axis=1, tiled=True)  21 us
  transfers between devices with their start and end apart: 14, of which 11 were waited for; matrix products, arithmetic and copies ran while one was open for 31% of the time, Pallas kernels for 0%

commit v1 on v0

--- a/solution.py
+++ b/solution.py
@@ -3,8 +3,233 @@
 
 import jax
 import jax.numpy as jnp
+import ml_dtypes
+import numpy as np
 from jax import lax
+from jax.experimental import pallas as pl
+from jax.experimental.pallas import tpu as pltpu
 from jax.sharding import PartitionSpec as P
+
+MESH = pl.DeviceIdType.MESH
+SIDE = 256
+LANES = 128
+
+
+def halves(table):
+    high = table.astype(ml_dtypes.bfloat16)
+    low = (table - high.astype(np.float64)).astype(ml_dtypes.bfloat16)
+    return (high, low)
+
+
+def fourier_tables():
+    total = SIDE * SIDE
+    index = np.arange(SIDE, dtype=np.float64)
+    outer = 2.0 * np.pi * np.outer(index + 0.25, index) / SIDE
+    first = np.concatenate([np.cos(outer), -np.sin(outer)], axis=0)
+    last = first.T / total
+    inner = 2.0 * np.pi * (np.outer(index, index) % SIDE) / SIDE
+    cosine, sine = np.cos(inner), np.sin(inner)
+    middle = np.block([[cosine, -sine], [sine, cosine]])
+    back = middle.T
+    twist = 2.0 * np.pi * np.outer(index + 0.25, index) / total
+    return (
+        *halves(first),
+        *halves(middle),
+        *halves(back),
+        *halves(last),
+        np.cos(twist).astype(np.float32),
+        (-np.sin(twist)).astype(np.float32),
+    )
+
+
+def split(value):
+    high = value.astype(jnp.bfloat16)
+    low = (value - high.astype(jnp.float32)).astype(jnp.bfloat16)
+    return high, low
+
+
+def mul(left, right):
+    dot = partial(jnp.dot, preferred_element_type=jnp.float32)
+    return dot(left[0], right[0]) + (dot(left[0], right[1]) + dot(left[1], right[0]))
+
+
+def row_kernel(
+    blocks, groups, k_ref, v_ref, q_ref, c_ref, taps_ref,
+    t0, t1, t2, t3, t4, t5, t6, t7, t8, t9, out_ref,
+    pieces, tap_pieces, rows, filt, result, back,
+    first_hi, first_lo, mid_hi, mid_lo, inv_hi, inv_lo, last_hi, last_lo, twist_re, twist_im,
+    table_sem, tap_send, tap_recv, slab_send, slab_recv, in_send, in_recv, out_send, out_recv,
+):
+    me = lax.axis_index("seq")
+    col = lax.axis_index("chan")
+    count = k_ref.shape[0]
+
+    held = (first_hi, first_lo, mid_hi, mid_lo, inv_hi, inv_lo, last_hi, last_lo, twist_re, twist_im)
+    loads = [
+        pltpu.make_async_copy(source, target, table_sem.at[place])
+        for place, (source, target) in enumerate(zip((t0, t1, t2, t3, t4, t5, t6, t7, t8, t9), held))
+    ]
+    for load in loads:
+        load.start()
+
+    barrier = pltpu.get_barrier_semaphore()
+    for step in range(1, blocks):
+        pl.semaphore_signal(barrier, inc=1, device_id=(lax.rem(me + step, blocks), col), device_id_type=MESH)
+    for step in range(1, groups):
+        pl.semaphore_signal(barrier, inc=1, device_id=(me, lax.rem(col + step, groups)), device_id_type=MESH)
+
+    for row in range(taps_ref.shape[1] // SIDE):
+        for half in range(SIDE // LANES):
+            tokens = slice(row * SIDE + half * LANES, row * SIDE + (half + 1) * LANES)
+            lanes = slice(half * LANES, (half + 1) * LANES)
+            tap_pieces[:, row, lanes] = taps_ref[:, tokens]
+    for row in range(k_ref.shape[1] // SIDE):
+        for half in range(SIDE // LANES):
+            tokens = slice(row * SIDE + half * LANES, row * SIDE + (half + 1) * LANES)
+            lanes = slice(half * LANES, (half + 1) * LANES)
+            pieces[:count, row, lanes] = k_ref[:, tokens] * v_ref[:, tokens]
+            pieces[count:, row, lanes] = c_ref[:, tokens] * q_ref[:, tokens]
+
+    pl.semaphore_wait(barrier, blocks + groups - 2)
+
+    tap_copies, in_copies = [], []
+    for step in range(1, blocks):
+        target = lax.rem(me + step, blocks)
+        copy = pltpu.make_async_remote_copy(
+            src_ref=tap_pieces.at[lax.rem(target, count)], dst_ref=filt.at[me, col],
+            send_sem=tap_send.at[step], recv_sem=tap_recv.at[step],
+            device_id=(target, col), device_id_type=MESH,
+        )
+        copy.start()
+        tap_copies.append(copy)
+    for step in range(1, blocks):
+        target = lax.rem(me + step, blocks)
+        copy = pltpu.make_async_remote_copy(
+            src_ref=pieces.at[target], dst_ref=rows.at[me],
+            send_sem=in_send.at[step], recv_sem=in_recv.at[step],
+            device_id=(target, col), device_id_type=MESH,
+        )
+        copy.start()
+        in_copies.append(copy)
+    filt[me, col] = tap_pieces[lax.rem(me, count)]
+    rows[me] = pieces[me]
+
+    for copy in tap_copies:
+        copy.wait_recv()
+    slab_copies = []
+    for step in range(1, groups):
+        copy = pltpu.make_async_remote_copy(
+            src_ref=filt.at[:, col], dst_ref=filt.at[:, col],
+            send_sem=slab_send.at[step], recv_sem=slab_recv.at[step],
+            device_id=(me, lax.rem(col + step, groups)), device_id_type=MESH,
+        )
+        copy.start()
+        slab_copies.append(copy)
+
+    for load in loads:
+        load.wait()
+
+    def spectrum(signal):
+        mixed = mul((first_hi[...], first_lo[...]), split(signal))
+        real, imag = mixed[:SIDE], mixed[SIDE:]
+        turn_re, turn_im = twist_re[...], twist_im[...]
+        twisted = jnp.concatenate(
+            [real * turn_re - imag * turn_im, real * turn_im + imag * turn_re], axis=1
+        )
+        fine = mul(split(twisted), (mid_hi[...], mid_lo[...]))
+        return fine[:, :SIDE], fine[:, SIDE:]
+
+    for copy in in_copies:
+        copy.wait_recv()
+    row_re, row_im = spectrum(rows[...].reshape(SIDE, SIDE))
+    for copy in slab_copies:
+        copy.wait_recv()
+    tap_re, tap_im = spectrum(filt[...].reshape(SIDE, SIDE))
+    tap_im = tap_im * jnp.where(me < count, 1.0, -1.0)
+    joined = jnp.concatenate(
+        [row_re * tap_re - row_im * tap_im, row_re * tap_im + row_im * tap_re], axis=1
+    )
+    coarse = mul(split(joined), (inv_hi[...], inv_lo[...]))
+    real, imag = coarse[:, :SIDE], coarse[:, SIDE:]
+    turn_re, turn_im = twist_re[...], twist_im[...]
+    level = jnp.concatenate(
+        [real * turn_re + imag * turn_im, imag * turn_re - real * turn_im], axis=0
+    )
+    rebuilt = mul((last_hi[...], last_lo[...]), split(level))
+    result[...] = rebuilt.reshape(result.shape)
+
+    out_copies = []
+    for step in range(1, blocks):
+        target = lax.rem(me + step, blocks)
+        copy = pltpu.make_async_remote_copy(
+            src_ref=result.at[target], dst_ref=back.at[me],
+            send_sem=out_send.at[step], recv_sem=out_recv.at[step],
+            device_id=(target, col), device_id_type=MESH,
+        )
+        copy.start()
+        out_copies.append(copy)
+    back[me] = result[me]
+    for copy in out_copies:
+        copy.wait_recv()
+    for row in range(back.shape[1]):
+        for half in range(SIDE // LANES):
+            tokens = slice(row * SIDE + half * LANES, row * SIDE + (half + 1) * LANES)
+            lanes = slice(half * LANES, (half + 1) * LANES)
+            out_ref[:, tokens] = back[:, row, lanes]
+    for copy in tap_copies + in_copies + slab_copies + out_copies:
+        copy.wait_send()
+
+
+def rows_on_device(query_gate, key_gate, value_input, filter_taps, cotangent):
+    count, width = query_gate.shape
+    blocks = lax.axis_size("seq")
+    groups = lax.axis_size("chan")
+    high = width // SIDE
+    tables = fourier_tables()
+    f32, bf16 = jnp.float32, jnp.bfloat16
+    any_space = pl.BlockSpec(memory_space=pl.ANY)
+    vmem = pl.BlockSpec(memory_space=pltpu.VMEM)
+    sums = pl.pallas_call(
+        partial(row_kernel, blocks, groups),
+        out_shape=jax.ShapeDtypeStruct((blocks, width), f32),
+        in_specs=[vmem] * 5 + [any_space] * len(tables),
+        out_specs=vmem,
+        scratch_shapes=[
+            pltpu.VMEM((blocks, high, SIDE), f32),
+            pltpu.VMEM((count, high // groups, SIDE), f32),
+            pltpu.VMEM((blocks, high, SIDE), f32),
+            pltpu.VMEM((blocks, groups, high // groups, SIDE), f32),
+            pltpu.VMEM((blocks, high, SIDE), f32),
+            pltpu.VMEM((blocks, high, SIDE), f32),
+            *[pltpu.VMEM(table.shape, bf16 if place < 8 else f32) for place, table in enumerate(tables)],
+            pltpu.SemaphoreType.DMA((len(tables),)),
+            pltpu.SemaphoreType.DMA((blocks,)),
+            pltpu.SemaphoreType.DMA((blocks,)),
+            pltpu.SemaphoreType.DMA((groups,)),
+            pltpu.SemaphoreType.DMA((groups,)),
+            pltpu.SemaphoreType.DMA((blocks,)),
+            pltpu.SemaphoreType.DMA((blocks,)),
+            pltpu.SemaphoreType.DMA((blocks,)),
+            pltpu.SemaphoreType.DMA((blocks,)),
+        ],
+        compiler_params=pltpu.CompilerParams(
+            collective_id=0, has_side_effects=True, vmem_limit_bytes=32 * 1024 * 1024
+        ),
+    )(key_gate, value_input, query_gate, cotangent, filter_taps, *[jnp.asarray(table) for table in tables])
+    convolved, gated_grad = sums[:count], sums[count:]
+    return (cotangent * convolved, gated_grad * value_input, gated_grad * key_gate)
+
+
+def one_row_each(query_gate, filter_taps):
+    count, width = query_gate.shape
+    blocks = lax.axis_size("seq")
+    groups = lax.axis_size("chan")
+    return (
+        blocks == 2 * count
+        and filter_taps.shape[0] == count
+        and blocks * width == SIDE * SIDE
+        and width % (8 * groups * SIDE) == 0
+    )
 
 
 def phase_table(row_count, column_count, offset, period, direction):
@@ -107,6 +332,8 @@
 
 
 def on_device(query_gate, key_gate, value_input, filter_taps, cotangent):
+    if one_row_each(query_gate, filter_taps):
+        return rows_on_device(query_gate, key_gate, value_input, filter_taps, cotangent)
     block_taps = lax.all_gather(filter_taps, "chan", axis=1, tiled=True)
     filter_real, filter_imag = forward_spectrum(block_taps)
     gated = key_gate * value_input

time: 550 us -> 40.3 us (0.07); the launches traced: 543 us -> 39.6 us
  matrix products: 380 us -> 0 us
  waiting for transfers between devices: 64.1 us -> 0 us
  starting transfers between devices: 63.9 us -> 0 us
  Pallas kernels: 0 us -> 23.9 us
  blocking collectives: 18.5 us -> 0 us
    dot_general x50 -> x0, matrix products: 380 us -> none  [the longest x10 94.2 us: complex_mix(): product(table_imag, data_imag)]
    all_to_all x14 -> x0, waiting for transfers between devices: 64.1 us -> none  [the longest x5 24.3 us: regroup_tokens(): lax.all_to_all(signal, 'seq', split_axis=1, concat_axis=1, tiled=True)]
    all_to_all x14 -> x0, starting transfers between devices: 63.9 us -> none  [the longest x5 23.3 us: regroup_tokens(): lax.all_to_all(signal, 'seq', split_axis=1, concat_axis=1, tiled=True)]
    pallas_call x0 -> x1, Pallas kernels: none -> 23.9 us  [rows_on_device(): pl.pallas_call(partial(row_kernel, blocks, groups), out_shape=jax.ShapeDt...]
    unnamed x10 -> x30, local copies, waits for them, and re-layouts: 0.02 us -> 14.2 us
    all_to_all x1 -> x0, blocking collectives: 12.7 us -> none  [regroup_spectrum(): lax.all_to_all(part_imag, 'seq', split_axis=1, concat_axis=1, tiled=True)]
    all_gather x1 -> x0, blocking collectives: 5.87 us -> none  [on_device(): block_taps = lax.all_gather(filter_taps, 'chan', axis=1, tiled=True)]
  transfers between devices with their start and end apart: 14 -> 0, of which waited for: 11 -> 0; matrix products, arithmetic and copies ran while one was open for 31% -> 0% of each run, Pallas kernels for 0% -> 0%
where the time goes in v1:
time: 40.3 us; the launch traced here: 39.6 us
  Pallas kernels  23.9 us (59%)
  local copies, waits for them, and re-layouts  14.2 us (35%)
  other arithmetic  0.81 us (2%)
  between operations  0.66 us (2%)
    pallas_call x1, Pallas kernels, rows_on_device(): pl.pallas_call(partial(row_kernel, blocks, groups), out_shape=jax.ShapeDt...  23.9 us
    unnamed x30, local copies, waits for them, and re-layouts  14.2 us
    mul x1, other arithmetic, rows_on_device(): gated_grad * key_gate  0.81 us

profile of v1, /device:TPU:0, one launch (start us, length us, event | category | flops | bytes accessed | tf_op | source)
XLA Modules:
  0.0 39.6 jit_solution(18325655360930231245)
XLA Ops:
  0.6 0.0 copy-start
  0.6 1.0 %copy-done = bf16[512,512]{1,0:T(8,128)(2,1)S(1)} copy-done((bf16[512,512]{1,0:T(8,128)(2,1)S(1)}, bf16[512,512]{1,0:T(8,128)(2,1)}, u32[]{:S(2)}) %copy-start) | copy-done | bytes 524312
  1.7 0.0 copy-start.1
  1.7 1.0 %copy-done.1 = bf16[512,512]{1,0:T(8,128)(2,1)S(1)} copy-done((bf16[512,512]{1,0:T(8,128)(2,1)S(1)}, bf16[512,512]{1,0:T(8,128)(2,1)}, u32[]{:S(2)}) %copy-start.1) | copy-done | bytes 524312
  2.7 0.0 copy-start.2
  2.7 1.0 %copy-done.2 = bf16[512,512]{1,0:T(8,128)(2,1)S(1)} copy-done((bf16[512,512]{1,0:T(8,128)(2,1)S(1)}, bf16[512,512]{1,0:T(8,128)(2,1)}, u32[]{:S(2)}) %copy-start.2) | copy-done | bytes 524312
  3.8 0.0 copy-start.3
  3.8 1.0 %copy-done.3 = bf16[512,512]{1,0:T(8,128)(2,1)S(1)} copy-done((bf16[512,512]{1,0:T(8,128)(2,1)S(1)}, bf16[512,512]{1,0:T(8,128)(2,1)}, u32[]{:S(2)}) %copy-start.3) | copy-done | bytes 524312
  4.8 0.0 copy-start.4
  4.8 0.9 %copy-done.4 = f32[4,8192]{1,0:T(4,128)S(1)} copy-done((f32[4,8192]{1,0:T(4,128)S(1)}, f32[4,8192]{1,0:T(4,128)}, u32[]{:S(2)}) %copy-start.4) | copy-done | bytes 131096
  5.7 0.0 copy-start.5
  5.7 0.9 %copy-done.5 = f32[4,8192]{1,0:T(4,128)S(1)} copy-done((f32[4,8192]{1,0:T(4,128)S(1)}, f32[4,8192]{1,0:T(4,128)}, u32[]{:S(2)}) %copy-start.5) | copy-done | bytes 131096
  6.6 0.0 copy-start.6
  6.6 0.9 %copy-done.6 = f32[4,8192]{1,0:T(4,128)S(1)} copy-done((f32[4,8192]{1,0:T(4,128)S(1)}, f32[4,8192]{1,0:T(4,128)}, u32[]{:S(2)}) %copy-start.6) | copy-done | bytes 131096
  7.5 0.9 %copy-done.7 = f32[256,256]{1,0:T(8,128)S(1)} copy-done((f32[256,256]{1,0:T(8,128)S(1)}, f32[256,256]{1,0:T(8,128)}, u32[]{:S(2)}) %copy-start.7) | copy-done | bytes 262168
  8.5 0.9 %copy-done.8 = f32[256,256]{1,0:T(8,128)S(1)} copy-done((f32[256,256]{1,0:T(8,128)S(1)}, f32[256,256]{1,0:T(8,128)}, u32[]{:S(2)}) %copy-start.8) | copy-done | bytes 262168
  9.4 0.9 %copy-done.9 = bf16[256,512]{1,0:T(8,128)(2,1)S(1)} copy-done((bf16[256,512]{1,0:T(8,128)(2,1)S(1)}, bf16[256,512]{1,0:T(8,128)(2,1)}, u32[]{:S(2)}) %copy-start.9) | copy-done | bytes 262168
  10.4 0.9 %copy-done.10 = bf16[256,512]{1,0:T(8,128)(2,1)S(1)} copy-done((bf16[256,512]{1,0:T(8,128)(2,1)S(1)}, bf16[256,512]{1,0:T(8,128)(2,1)}, u32[]{:S(2)}) %copy-start.10) | copy-done | bytes 262168
  11.3 0.9 %copy-done.11 = bf16[512,256]{1,0:T(8,128)(2,1)S(1)} copy-done((bf16[512,256]{1,0:T(8,128)(2,1)S(1)}, bf16[512,256]{1,0:T(8,128)(2,1)}, u32[]{:S(2)}) %copy-start.11) | copy-done | bytes 262168
  12.3 0.9 %copy-done.12 = bf16[512,256]{1,0:T(8,128)(2,1)S(1)} copy-done((bf16[512,256]{1,0:T(8,128)(2,1)S(1)}, bf16[512,256]{1,0:T(8,128)(2,1)}, u32[]{:S(2)}) %copy-start.12) | copy-done | bytes 262168
  13.2 0.9 %copy-done.13 = f32[4,8192]{1,0:T(4,128)S(1)} copy-done((f32[4,8192]{1,0:T(4,128)S(1)}, f32[4,8192]{1,0:T(4,128)}, u32[]{:S(2)}) %copy-start.13) | copy-done | bytes 131096
  14.1 0.8 %copy-done.14 = f32[4,2048]{1,0:T(4,128)S(1)} copy-done((f32[4,2048]{1,0:T(4,128)S(1)}, f32[4,2048]{1,0:T(4,128)}, u32[]{:S(2)}) %copy-start.14) | copy-done | bytes 32792
  14.9 23.9 %shard_map.166 = f32[8,8192]{1,0:T(8,128)S(1)} custom-call(f32[4,8192]{1,0:T(4,128)S(1)} %copy-done.4, f32[4,8192]{1,0:T(4,128)S(1)} %copy-done.5, f32[4,8192]{1,0:T(4,128)S(1)} %copy-done.13, f32[4,8192]{1,0:T(4,128)S(1)} %copy-done.6, f32[4,2048]{1,0:T(4,128)S(1)} %copy-done.14, bf16[512,256]{1,0:T(8,128)(2,1)S(1)} %copy-done.12, ...), custom_call_target="tpu_custom_call" | custom-call | tf_op jit(solution)/shard_map/pallas_call | solution.py:192
  38.8 0.8 %slice_multiply_fusion.1 = (f32[4,8192]{1,0:T(4,128)}, f32[4,8192]{1,0:T(4,128)}, f32[4,8192]{1,0:T(4,128)}) fusion(f32[4,8192]{1,0:T(4,128)S(1)} %copy-done.4, f32[8,8192]{1,0:T(8,128)S(1)} %shard_map.166, f32[4,8192]{1,0:T(4,128)S(1)} %copy-done.5, f32[4,8192]{1,0:T(4,128)S(1)} %copy-done.6), kind=kLoop, calls=%fused_computation.1 | loop fusion | flops 98304 | bytes 1048576 | tf_op jit(solution)/shard_map/mul | solution.py:220
  (8 shorter events, 0.0 us)
Async XLA Ops:
  0.6 1.0 %copy-start = (bf16[512,512]{1,0:T(8,128)(2,1)S(1)}, bf16[512,512]{1,0:T(8,128)(2,1)}, u32[]{:S(2)}) copy-start(bf16[512,512]{1,0:T(8,128)(2,1)} %constant.25.clone.t5) | copy-start | bytes 1572868
  1.7 1.0 %copy-start.1 = (bf16[512,512]{1,0:T(8,128)(2,1)S(1)}, bf16[512,512]{1,0:T(8,128)(2,1)}, u32[]{:S(2)}) copy-start(bf16[512,512]{1,0:T(8,128)(2,1)} %constant.24.clone.t4) | copy-start | bytes 1572868
  2.7 1.0 %copy-start.2 = (bf16[512,512]{1,0:T(8,128)(2,1)S(1)}, bf16[512,512]{1,0:T(8,128)(2,1)}, u32[]{:S(2)}) copy-start(bf16[512,512]{1,0:T(8,128)(2,1)} %constant.23.clone.t3) | copy-start | bytes 1572868
  3.8 1.0 %copy-start.3 = (bf16[512,512]{1,0:T(8,128)(2,1)S(1)}, bf16[512,512]{1,0:T(8,128)(2,1)}, u32[]{:S(2)}) copy-start(bf16[512,512]{1,0:T(8,128)(2,1)} %constant.22.clone.t2) | copy-start | bytes 1572868
  4.8 0.9 %copy-start.4 = (f32[4,8192]{1,0:T(4,128)S(1)}, f32[4,8192]{1,0:T(4,128)}, u32[]{:S(2)}) copy-start(f32[4,8192]{1,0:T(4,128)} %k_ref.1) | copy-start | bytes 393220
  5.7 0.9 %copy-start.5 = (f32[4,8192]{1,0:T(4,128)S(1)}, f32[4,8192]{1,0:T(4,128)}, u32[]{:S(2)}) copy-start(f32[4,8192]{1,0:T(4,128)} %v_ref.1) | copy-start | bytes 393220
  6.6 0.9 %copy-start.6 = (f32[4,8192]{1,0:T(4,128)S(1)}, f32[4,8192]{1,0:T(4,128)}, u32[]{:S(2)}) copy-start(f32[4,8192]{1,0:T(4,128)} %c_ref.1) | copy-start | bytes 393220
  7.5 0.9 %copy-start.7 = (f32[256,256]{1,0:T(8,128)S(1)}, f32[256,256]{1,0:T(8,128)}, u32[]{:S(2)}) copy-start(f32[256,256]{1,0:T(8,128)} %constant.29.clone.t9) | copy-start | bytes 786436
  8.5 0.9 %copy-start.8 = (f32[256,256]{1,0:T(8,128)S(1)}, f32[256,256]{1,0:T(8,128)}, u32[]{:S(2)}) copy-start(f32[256,256]{1,0:T(8,128)} %constant.28.clone.t8) | copy-start | bytes 786436
  9.4 0.9 %copy-start.9 = (bf16[256,512]{1,0:T(8,128)(2,1)S(1)}, bf16[256,512]{1,0:T(8,128)(2,1)}, u32[]{:S(2)}) copy-start(bf16[256,512]{1,0:T(8,128)(2,1)} %constant.27.clone.t7) | copy-start | bytes 786436
  10.4 0.9 %copy-start.10 = (bf16[256,512]{1,0:T(8,128)(2,1)S(1)}, bf16[256,512]{1,0:T(8,128)(2,1)}, u32[]{:S(2)}) copy-start(bf16[256,512]{1,0:T(8,128)(2,1)} %constant.26.clone.t6) | copy-start | bytes 786436
  11.3 0.9 %copy-start.11 = (bf16[512,256]{1,0:T(8,128)(2,1)S(1)}, bf16[512,256]{1,0:T(8,128)(2,1)}, u32[]{:S(2)}) copy-start(bf16[512,256]{1,0:T(8,128)(2,1)} %constant.21.clone.t1) | copy-start | bytes 786436
  12.3 0.9 %copy-start.12 = (bf16[512,256]{1,0:T(8,128)(2,1)S(1)}, bf16[512,256]{1,0:T(8,128)(2,1)}, u32[]{:S(2)}) copy-start(bf16[512,256]{1,0:T(8,128)(2,1)} %constant.20.clone.t0) | copy-start | bytes 786436
  13.2 0.9 %copy-start.13 = (f32[4,8192]{1,0:T(4,128)S(1)}, f32[4,8192]{1,0:T(4,128)}, u32[]{:S(2)}) copy-start(f32[4,8192]{1,0:T(4,128)} %q_ref.1) | copy-start | bytes 393220
  14.1 0.8 %copy-start.14 = (f32[4,2048]{1,0:T(4,128)S(1)}, f32[4,2048]{1,0:T(4,128)}, u32[]{:S(2)}) copy-start(f32[4,2048]{1,0:T(4,128)} %taps_ref.1) | copy-start | bytes 98308
